TPU v7x, 256 devices: a whole 4x4x8 slice. The times are simulated.
256 devices in a mesh: src: 32 (over y, x, core), tgt: 8 (over z).
Axes of the slice: x: 4, y: 4, z: 8, core: 2. Of those that a mesh axis runs over, the one named last changes fastest.
Arguments:
- src_points: bfloat16 [32, 524288], P(None, 'src'), may hold values from -24 to 24
- tgt_points: bfloat16 [32, 524288], P(None, 'tgt'), may hold values from -6 to 6
- tgt_potential: float32 [524288], P('tgt'), may hold values from -2 to 2
- support: int32 [4096, 8, 6], P('src', 'tgt'), may hold values from 0 to 511, as said below
- counts: int32 [4096, 8], P('src', 'tgt'), may hold values from 1 to 6, as said below
Outputs:
- src_potential: float32 [524288], P('src')
- new_tgt_potential: float32 [524288], P('tgt')
Inputs may be any that keep to these rules, and one draw needn't show every extreme that they name: support[r, t, k] names target block t * 512 + support[r, t, k]; the first counts[r, t] entries of a list are distinct; every target block is named in the used part of some list. `counts`: for every source block the list of some target shard is full.
All inputs are finite; a program needn't handle non-finite values.
Results may differ from a plain program's by a relative error of at most 0.0004.
Values sent between devices are 32-bit elements; how exact they have to be, the bound alone decides.
A program may use at most 128 MiB of HBM per device.

v0:
```python
import math
import jax
import jax.numpy as jnp
from jax import lax
from jax.sharding import PartitionSpec as P

BLK = 128
entropy_blur = 0.05
neg_fill = -1e30


def body(src_points, tgt_points, tgt_potential, support, counts):
    features = src_points.shape[0]
    src_count = src_points.shape[1]
    tgt_count = tgt_points.shape[1]
    src_blocks = src_count // BLK
    tgt_blocks = tgt_count // BLK
    slot_count = support.shape[2]
    total_src = src_count * lax.axis_size("src")
    total_tgt = tgt_count * lax.axis_size("tgt")
    per_step = math.gcd(src_blocks, 8)
    step_count = src_blocks // per_step
    block_lists = support[:, 0, :]
    live_slots = jnp.arange(slot_count, dtype=jnp.int32)[None, :] < counts[:, 0][:, None]
    src_sq = jnp.sum(jnp.square(src_points.astype(jnp.float32)), axis=0).reshape(src_blocks, BLK)
    tgt_cube = tgt_points.reshape(features, tgt_blocks, BLK)
    tgt_sq = jnp.sum(jnp.square(tgt_points.astype(jnp.float32)), axis=0).reshape(tgt_blocks, BLK)
    tgt_pot = tgt_potential.reshape(tgt_blocks, BLK)

    def group_cost(step_index):
        first_block = step_index * per_step
        src_rows = lax.dynamic_slice_in_dim(src_points, first_block * BLK, per_step * BLK, 1)
        src_rows = src_rows.reshape(features, per_step, BLK)
        picked = lax.dynamic_slice_in_dim(block_lists, first_block, per_step, 0)
        live_mask = lax.dynamic_slice_in_dim(live_slots, first_block, per_step, 0)
        rows_sq = lax.dynamic_slice_in_dim(src_sq, first_block, per_step, 0)
        near_points = jnp.take(tgt_cube, picked.reshape(-1), axis=1).reshape(
            features, per_step, slot_count, BLK
        )
        inner_prod = jnp.einsum(
            "dgi,dgkj->gikj", src_rows, near_points, preferred_element_type=jnp.float32
        )
        cost_tile = (rows_sq[:, :, None, None] + tgt_sq[picked][:, None, :, :]) / (
            2.0 * features
        ) - inner_prod / features
        return (cost_tile, picked, live_mask)

    def row_part(step_index):
        cost_tile, picked, live_mask = group_cost(step_index)
        row_score = jnp.where(
            live_mask[:, None, :, None],
            (tgt_pot[picked][:, None, :, :] - cost_tile) / entropy_blur,
            neg_fill,
        )
        highest = jnp.max(row_score, axis=(2, 3))
        summed = jnp.sum(jnp.exp(row_score - highest[:, :, None, None]), axis=(2, 3))
        return (highest, summed)

    row_high, row_total = lax.map(row_part, jnp.arange(step_count, dtype=jnp.int32))
    row_high = row_high.reshape(src_count)
    row_total = row_total.reshape(src_count)
    global_high = lax.pmax(row_high, "tgt")
    row_total = lax.psum(row_total * jnp.exp(row_high - global_high), "tgt")
    row_high = global_high
    src_potential = -entropy_blur * (row_high + jnp.log(row_total) - math.log(total_tgt))
    src_pot = src_potential.reshape(src_blocks, BLK)

    def col_part(step_index):
        cost_tile, picked, live_mask = group_cost(step_index)
        block_pot = lax.dynamic_slice_in_dim(src_pot, step_index * per_step, per_step, 0)
        col_score = jnp.where(
            live_mask[:, None, :, None],
            (block_pot[:, :, None, None] - cost_tile) / entropy_blur,
            neg_fill,
        )
        highest = jnp.max(col_score, axis=1)
        summed = jnp.sum(jnp.exp(col_score - highest[:, None]), axis=1)
        return (highest, summed)

    tile_high, tile_total = lax.map(col_part, jnp.arange(step_count, dtype=jnp.int32))
    tile_high = tile_high.reshape(src_blocks * slot_count, BLK)
    tile_total = tile_total.reshape(src_blocks * slot_count, BLK)
    owners = jnp.where(live_slots, block_lists, tgt_blocks).reshape(-1)
    seg_high = jax.ops.segment_max(tile_high, owners, num_segments=tgt_blocks + 1)
    seg_total = jax.ops.segment_sum(
        tile_total * jnp.exp(tile_high - seg_high[owners]), owners, num_segments=tgt_blocks + 1
    )
    col_high = jnp.maximum(seg_high[:tgt_blocks], neg_fill).reshape(tgt_count)
    col_total = seg_total[:tgt_blocks].reshape(tgt_count)
    global_high = lax.pmax(col_high, "src")
    global_total = lax.psum(col_total * jnp.exp(col_high - global_high), "src")
    new_tgt_potential = -entropy_blur * (global_high + jnp.log(global_total) - math.log(total_src))
    return (src_potential, new_tgt_potential)


def solution(mesh):
    return jax.shard_map(
        body,
        mesh=mesh,
        in_specs=(P(None, "src"), P(None, "tgt"), P("tgt"), P("src", "tgt", None), P("src", "tgt")),
        out_specs=(P("src"), P("tgt")),
        check_vma=False,
    )
```

profile of v0, /device:TPU:1, one launch (start us, length us, event | category | flops | bytes accessed | tf_op | source)
XLA Modules:
  0.0 693.1 jit_solution(16128332528436720844)
XLA Ops:
  7.2 5.0 copy_bitcast_fusion
  14.0 156.2 %while.28 = (s32[]{:T(128)}, f32[16,8,128]{2,1,0:T(8,128)S(1)}, f32[16,8,128]{2,1,0:T(8,128)S(1)}, s32[16]{0:T(128)S(1)}, pred[128,6]{1,0:T(8,128)(4,1)S(1)}, /*...) while((s32[]{:T(128)}, f32[16,8,128]{2,1,0:T(8,128)S(1)}, ...), condition=%wide.region_5.7_spmd, body=%wide.region_2.6_spmd.sunk | while | flops 58393160 | bytes 8883529 | solution.py:59
  15.4 2.8 gather_fusion
  20.4 3.0 fusion.24
  25.2 2.8 gather_fusion
  30.1 3.0 fusion.24
  34.9 2.8 gather_fusion
  39.9 3.0 fusion.24
  44.7 2.8 gather_fusion
  49.7 3.0 fusion.24
  54.5 2.8 gather_fusion
  59.4 3.0 fusion.24
  64.2 2.8 gather_fusion
  69.2 3.0 fusion.24
  74.0 2.8 gather_fusion
  79.0 3.0 fusion.24
  83.7 2.8 gather_fusion
  88.7 3.0 fusion.24
  93.5 2.8 gather_fusion
  98.5 3.0 fusion.24
  103.3 2.8 gather_fusion
  108.2 3.0 fusion.24
  113.0 2.8 gather_fusion
  118.0 3.0 fusion.24
  122.8 2.8 gather_fusion
  127.8 3.0 fusion.24
  132.5 2.8 gather_fusion
  137.5 3.0 fusion.24
  142.3 2.8 gather_fusion
  147.3 3.0 fusion.24
  152.1 2.8 gather_fusion
  157.0 3.0 fusion.24
  161.8 2.8 gather_fusion
  166.8 3.0 fusion.24
  171.3 70.0 %all-reduce.5.cloned.1.call-done = f32[16384]{0:T(1024)} async-done(((f32[16384]{0:T(1024)}), f32[16384]{0:T(1024)}) %all-reduce.5.cloned.1.call-update) | async-done | bytes 65552 | tf_op jit(solution)/shard_map/pmax | solution.py:62
  242.8 71.3 %all-reduce.7.cloned.1.call-done = f32[16384]{0:T(1024)} async-done(((f32[16384]{0:T(1024)}), f32[16384]{0:T(1024)}) %all-reduce.7.cloned.1.call-update) | async-done | bytes 65552 | tf_op jit(solution)/shard_map/psum | solution.py:63
  315.0 133.0 %while.29 = (s32[]{:T(128)}, f32[16,8,6,128]{3,2,1,0:T(8,128)S(1)}, f32[16,8,6,128]{3,2,1,0:T(8,128)S(1)}, s32[16]{0:T(128)S(1)}, pred[128,6]{1,0:T(8,128)(4,1)S...) while((s32[]{:T(128)}, f32[16,8,6,128]{3,2,1,0:T(8,128)S(1)}, ...), condition=%wide.region_11.13_spmd, body=%wide.region_8.12_spmd.sunk | while | flops 58382920 | bytes 8948877 | solution.py:80
  316.4 2.8 gather_fusion.3
  320.8 1.8 fusion.26
  324.7 2.8 gather_fusion.3
  329.1 1.8 fusion.26
  333.0 2.8 gather_fusion.3
  337.4 1.8 fusion.26
  341.3 2.8 gather_fusion.3
  345.7 1.8 fusion.26
  349.6 2.8 gather_fusion.3
  357.9 2.8 gather_fusion.3
  362.3 1.8 fusion.26
  366.3 2.8 gather_fusion.3
  370.6 1.8 fusion.26
  374.6 2.8 gather_fusion.3
  382.9 2.8 gather_fusion.3
  391.2 2.8 gather_fusion.3
  395.6 1.8 fusion.26
  399.5 2.8 gather_fusion.3
  407.8 2.8 gather_fusion.3
  416.1 2.8 gather_fusion.3
  424.5 2.8 gather_fusion.3
  432.8 2.8 gather_fusion.3
  441.1 2.8 gather_fusion.3
  448.1 6.1 scatter_custom_fusion
  455.2 9.2 %scatter_custom_fusion.1 = f32[513,128]{1,0:T(8,128)S(1)} fusion(s32[768]{0:T(1024)S(1)} %get-tuple-element.306, f32[768,128]{1,0:T(8,128)S(1)} %reshape.162, f32[768,128]{1,0:T(8,128)S(1)} %reshape.216, f32[]{:T(128)} %constant.183.clone.1, f32[513,128]{1,0:T(8,128)S(1)} %scatter_custom_fusion, s32[1024]{0:T(1024)S(1)} %pad_clamp_fusion.4), kind=kCustom, calls=%fused_computation.42 | custom fusion | flops 294912 | bytes 1319428 | tf_op jit(solution)/shard_map/scatter-add | solution.py:85
  464.4 105.5 %all-reduce.9.cloned.1.call-done = f32[65536]{0:T(1024)} async-done(((f32[65536]{0:T(1024)}), f32[65536]{0:T(1024)}) %all-reduce.9.cloned.1.call-update) | async-done | bytes 262160 | tf_op jit(solution)/shard_map/pmax | solution.py:90
  571.7 113.1 %all-reduce.11.cloned.1.call-done = f32[65536]{0:T(1024)} async-done(((f32[65536]{0:T(1024)}), f32[65536]{0:T(1024)}) %all-reduce.11.cloned.1.call-update) | async-done | bytes 262160 | tf_op jit(solution)/shard_map/psum | solution.py:91
  (644 shorter events, 103.8 us)
Async XLA Ops:
  7.2 234.0 %all-reduce.5.cloned.1.call-start = ((), (), s32[]{:S(2)}) async-start(), calls=%async_computation | async-start | bytes 131072 | tf_op jit(solution)/shard_map/pmax | solution.py:62
  7.2 5.0 copy-start
  12.2 1.3 copy-start.5
  12.2 1.4 copy-start.6
  12.2 1.5 copy-start.2
  12.2 1.8 copy-start.1
  170.2 0.6 copy-start.3
  170.9 143.2 %all-reduce.7.cloned.1.call-start = ((), (), s32[]{:S(2)}) async-start(), calls=%async_computation.1 | async-start | bytes 131072 | tf_op jit(solution)/shard_map/psum | solution.py:63
  242.8 327.2 %all-reduce.9.cloned.1.call-start = ((), (), s32[]{:S(2)}) async-start(), calls=%async_computation.2 | async-start | bytes 524288 | tf_op jit(solution)/shard_map/pmax | solution.py:90
  448.0 238.6 %copy-start.4 = (f32[128,128]{1,0:T(8,128)}, f32[128,128]{1,0:T(8,128)S(1)}, u32[]{:S(2)}) copy-start(f32[128,128]{1,0:T(8,128)S(1)} %get-tuple-element.643) | copy-start | bytes 196612
  454.9 229.9 %all-reduce.11.cloned.1.call-start = ((), (), s32[]{:S(2)}) async-start(), calls=%async_computation.3 | async-start | bytes 524288 | tf_op jit(solution)/shard_map/psum | solution.py:91
Sparse Core Ops, SparseCore 0:
  171.0 70.1 all-reduce.4
  244.2 69.8 all-reduce.6
  455.0 114.8 all-reduce.8
  573.6 111.1 all-reduce.10
where the time goes:
time: 695 us; the launch traced here: 693 us
  waiting for transfers between devices  360 us (52%)
  local copies, waits for them, and re-layouts  150 us (22%)
  matrix products  76.1 us (11%)
  other arithmetic  47.1 us (7%)
  loops' own time  45.3 us (7%)
  between operations  14 us (2%)
    psum x1, waiting for transfers between devices, body(): global_total = lax.psum(col_total * jnp.exp(col_high - global_high), 'src')  113 us
    pmax x1, waiting for transfers between devices, body(): global_high = lax.pmax(col_high, 'src')  106 us
    gather x32, local copies, waits for them, and re-layouts, group_cost(): jnp.take(tgt_cube, picked.reshape(-1), axis=1)  90 us
    dot_general x32, matrix products, group_cost(): jnp.einsum('dgi,dgkj->gikj', src_rows, near_points, preferred_element_typ...  76.1 us
    psum x1, waiting for transfers between devices, body(): row_total = lax.psum(row_total * jnp.exp(row_high - global_high), 'tgt')  71.3 us
    pmax x1, waiting for transfers between devices, body(): global_high = lax.pmax(row_high, 'tgt')  70 us
    another operation x1, loops' own time, body(): lax.map(col_part, jnp.arange(step_count, dtype=jnp.int32))  22.7 us
    another operation x1, loops' own time, body(): lax.map(row_part, jnp.arange(step_count, dtype=jnp.int32))  22.6 us
  transfers between devices with their start and end apart: 4, of which 4 were waited for; matrix products, arithmetic and copies ran while one was open for 1% of the time, Pallas kernels for 0%

commit v1 on v0

--- a/solution.py
+++ b/solution.py
@@ -88,7 +88,9 @@
     col_high = jnp.maximum(seg_high[:tgt_blocks], neg_fill).reshape(tgt_count)
     col_total = seg_total[:tgt_blocks].reshape(tgt_count)
     global_high = lax.pmax(col_high, "src")
-    global_total = lax.psum(col_total * jnp.exp(col_high - global_high), "src")
+    global_total = jnp.sum(
+        lax.all_gather(col_total * jnp.exp(col_high - global_high), "src"), axis=0
+    )
     new_tgt_potential = -entropy_blur * (global_high + jnp.log(global_total) - math.log(total_src))
     return (src_potential, new_tgt_potential)
 

time: 695 us -> 652 us (0.938)
  waiting for transfers between devices: 360 us -> 306 us
    psum x1 -> x0, waiting for transfers between devices: 113 us -> none  [body(): global_total = lax.psum(col_total * jnp.exp(col_high - global_high), 'src')]
    all_gather x0 -> x1, waiting for transfers between devices: none -> 59.5 us  [body(): lax.all_gather(col_total * jnp.exp(col_high - global_high), 'src')]
    all_gather x0 -> x1, local copies, waits for them, and re-layouts: none -> 7.47 us  [body(): lax.all_gather(col_total * jnp.exp(col_high - global_high), 'src')]
where the time goes in v1:
time: 652 us; the launch traced here: 650 us
  waiting for transfers between devices  306 us (47%)
  local copies, waits for them, and re-layouts  156 us (24%)
  matrix products  76 us (12%)
  other arithmetic  52.7 us (8%)
  loops' own time  45.4 us (7%)
  between operations  14 us (2%)
    pmax x1, waiting for transfers between devices, body(): global_high = lax.pmax(col_high, 'src')  106 us
    gather x32, local copies, waits for them, and re-layouts, group_cost(): jnp.take(tgt_cube, picked.reshape(-1), axis=1)  90 us
    dot_general x32, matrix products, group_cost(): jnp.einsum('dgi,dgkj->gikj', src_rows, near_points, preferred_element_typ...  76 us
    psum x1, waiting for transfers between devices, body(): row_total = lax.psum(row_total * jnp.exp(row_high - global_high), 'tgt')  71.3 us
    pmax x1, waiting for transfers between devices, body(): global_high = lax.pmax(row_high, 'tgt')  70 us
    all_gather x1, waiting for transfers between devices, body(): lax.all_gather(col_total * jnp.exp(col_high - global_high), 'src')  59.5 us
    another operation x1, loops' own time, body(): lax.map(col_part, jnp.arange(step_count, dtype=jnp.int32))  22.7 us
    another operation x1, loops' own time, body(): lax.map(row_part, jnp.arange(step_count, dtype=jnp.int32))  22.7 us
  transfers between devices with their start and end apart: 4, of which 4 were waited for; matrix products, arithmetic and copies ran while one was open for 1% of the time, Pallas kernels for 0%

profile of v1, /device:TPU:1, one launch (start us, length us, event | category | flops | bytes accessed | tf_op | source)
XLA Modules:
  0.0 650.2 jit_solution(9754515273704020955)
XLA Ops:
  7.2 3.6 multiply_reduce_fusion
  10.9 2.6 copy_bitcast_fusion
  14.1 156.2 %while.28 = (s32[]{:T(128)}, f32[16,8,128]{2,1,0:T(8,128)S(1)}, f32[16,8,128]{2,1,0:T(8,128)S(1)}, s32[16]{0:T(128)S(1)}, pred[128,6]{1,0:T(8,128)(4,1)S(1)}, /*...) while((s32[]{:T(128)}, f32[16,8,128]{2,1,0:T(8,128)S(1)}, ...), condition=%wide.region_5.7_spmd, body=%wide.region_2.6_spmd.sunk | while | flops 58393160 | bytes 8883537 | solution.py:59
  17.5 2.8 gather_fusion
  20.4 3.0 fusion.24
  27.2 2.8 gather_fusion
  30.2 3.0 fusion.24
  37.0 2.8 gather_fusion
  39.9 3.0 fusion.24
  46.7 2.8 gather_fusion
  49.7 3.0 fusion.24
  56.5 2.8 gather_fusion
  59.5 3.0 fusion.24
  66.3 2.8 gather_fusion
  69.2 3.0 fusion.24
  76.0 2.8 gather_fusion
  79.0 3.0 fusion.24
  85.8 2.8 gather_fusion
  88.7 3.0 fusion.24
  95.5 2.8 gather_fusion
  98.5 3.0 fusion.24
  105.3 2.8 gather_fusion
  108.3 3.0 fusion.24
  115.1 2.8 gather_fusion
  118.0 3.0 fusion.24
  124.8 2.8 gather_fusion
  127.8 3.0 fusion.24
  134.6 2.8 gather_fusion
  137.5 3.0 fusion.24
  144.3 2.8 gather_fusion
  147.3 3.0 fusion.24
  154.1 2.8 gather_fusion
  157.1 3.0 fusion.24
  163.9 2.8 gather_fusion
  166.8 3.0 fusion.24
  171.3 70.0 %all-reduce.4.cloned.1.call-done = f32[16384]{0:T(1024)} async-done(((f32[16384]{0:T(1024)}), f32[16384]{0:T(1024)}) %all-reduce.4.cloned.1.call-update) | async-done | bytes 65552 | tf_op jit(solution)/shard_map/pmax | solution.py:62
  242.8 71.3 %all-reduce.6.cloned.1.call-done = f32[16384]{0:T(1024)} async-done(((f32[16384]{0:T(1024)}), f32[16384]{0:T(1024)}) %all-reduce.6.cloned.1.call-update) | async-done | bytes 65552 | tf_op jit(solution)/shard_map/psum | solution.py:63
  315.0 133.0 %while.29 = (s32[]{:T(128)}, f32[16,8,6,128]{3,2,1,0:T(8,128)S(1)}, f32[16,8,6,128]{3,2,1,0:T(8,128)S(1)}, s32[16]{0:T(128)S(1)}, pred[128,6]{1,0:T(8,128)(4,1)S...) while((s32[]{:T(128)}, f32[16,8,6,128]{3,2,1,0:T(8,128)S(1)}, ...), condition=%wide.region_11.13_spmd, body=%wide.region_8.12_spmd.sunk | while | flops 58382920 | bytes 8948885 | solution.py:80
  317.8 2.8 gather_fusion.3
  320.8 1.8 fusion.26
  326.1 2.8 gather_fusion.3
  329.1 1.8 fusion.26
  334.5 2.8 gather_fusion.3
  342.8 2.8 gather_fusion.3
  351.1 2.8 gather_fusion.3
  359.4 2.8 gather_fusion.3
  367.7 2.8 gather_fusion.3
  376.0 2.8 gather_fusion.3
  379.0 1.8 fusion.26
  384.3 2.8 gather_fusion.3
  387.3 1.8 fusion.26
  392.6 2.8 gather_fusion.3
  400.9 2.8 gather_fusion.3
  409.3 2.8 gather_fusion.3
  417.6 2.8 gather_fusion.3
  425.9 2.8 gather_fusion.3
  434.2 2.8 gather_fusion.3
  442.5 2.8 gather_fusion.3
  448.1 6.1 scatter_custom_fusion
  455.2 9.2 %scatter_custom_fusion.1 = f32[513,128]{1,0:T(8,128)S(1)} fusion(s32[768]{0:T(1024)S(1)} %get-tuple-element.350, f32[768,128]{1,0:T(8,128)S(1)} %reshape.162, f32[768,128]{1,0:T(8,128)S(1)} %reshape.216, f32[]{:T(128)} %constant.183.clone.1, f32[513,128]{1,0:T(8,128)S(1)} %scatter_custom_fusion, s32[1024]{0:T(1024)S(1)} %pad_clamp_fusion.4), kind=kCustom, calls=%fused_computation.42 | custom fusion | flops 294912 | bytes 1319428 | tf_op jit(solution)/shard_map/scatter-add | solution.py:85
  464.4 105.5 %all-reduce.8.cloned.1.call-done = f32[65536]{0:T(1024)} async-done(((f32[65536]{0:T(1024)}), f32[65536]{0:T(1024)}) %all-reduce.8.cloned.1.call-update) | async-done | bytes 262160 | tf_op jit(solution)/shard_map/pmax | solution.py:90
  571.6 59.5 %all-gather.3.cloned.1.call-done = f32[2097152]{0:T(1024)} async-done(((f32[65536]{0:T(1024)}), f32[2097152]{0:T(1024)}) %all-gather.3.cloned.1.call-update) | async-done | bytes 8388624 | tf_op jit(solution)/shard_map/all_gather | solution.py:92
  631.1 7.5 %reshape.228 = f32[32,65536]{1,0:T(8,128)} reshape(f32[2097152]{0:T(1024)} %all-gather.3.cloned.1.call-done) | data formatting | bytes 16777216 | tf_op jit(solution)/shard_map/all_gather | solution.py:92
  638.6 4.3 reduce_sum.53
  (648 shorter events, 106.9 us)
Async XLA Ops:
  7.2 234.1 %all-reduce.4.cloned.1.call-start = ((), (), s32[]{:S(2)}) async-start(), calls=%async_computation | async-start | bytes 131072 | tf_op jit(solution)/shard_map/pmax | solution.py:62
  7.2 3.6 copy-start
  10.8 2.7 copy-start.7
  10.8 2.8 copy-start.6
  10.8 2.9 copy-start.2
  10.9 3.2 copy-start.1
  170.2 0.6 copy-start.4
  170.9 143.2 %all-reduce.6.cloned.1.call-start = ((), (), s32[]{:S(2)}) async-start(), calls=%async_computation.1 | async-start | bytes 131072 | tf_op jit(solution)/shard_map/psum | solution.py:63
  242.8 327.1 %all-reduce.8.cloned.1.call-start = ((), (), s32[]{:S(2)}) async-start(), calls=%async_computation.2 | async-start | bytes 524288 | tf_op jit(solution)/shard_map/pmax | solution.py:90
  448.0 190.6 %copy-start.5 = (f32[128,128]{1,0:T(8,128)}, f32[128,128]{1,0:T(8,128)S(1)}, u32[]{:S(2)}) copy-start(f32[128,128]{1,0:T(8,128)S(1)} %get-tuple-element.687) | copy-start | bytes 196612
  454.9 176.2 %all-gather.3.cloned.1.call-start = ((), (), s32[]{:S(2)}) async-start(), calls=%async_computation.3 | async-start | bytes 8650752 | tf_op jit(solution)/shard_map/all_gather | solution.py:92
  638.6 4.3 copy-start.3
Sparse Core Ops, SparseCore 0:
  171.0 70.1 all-reduce.3
  244.2 69.8 all-reduce.5
  455.0 114.8 all-reduce.7
  572.9 58.1 all-gather.2
